TPU v7x, 256 devices: a whole 4x4x8 slice. The times are simulated.
256 devices in a mesh: fsdp: 32 (over y, x, core), ctx: 8 (over z).
Axes of the slice: x: 4, y: 4, z: 8, core: 2. Of those that a mesh axis runs over, the one named last changes fastest.
Arguments:
- tokens: bfloat16 [16384, 8192], P('fsdp'), may hold values from -12 to 12
- wq: bfloat16 [8192, 4096], P('fsdp', 'ctx'), may hold values from -0.0625 to 0.0625
- wo: bfloat16 [4096, 8192], P('ctx', 'fsdp'), may hold values from -1.5 to 1.5
- key_cache: bfloat16 [65536, 1024], P(('fsdp', 'ctx')), may hold values from -500 to 500, as said below
- value_cache: bfloat16 [65536, 1024], P(('fsdp', 'ctx')), may hold values from -6 to 6
- key_blocks: int32 [32, 4, 8], P('fsdp'), may hold values from 0 to 15, as said below
Outputs:
- mixed: bfloat16 [16384, 8192], P('fsdp', 'ctx')
Inputs may be any that keep to these rules, and one draw needn't show every extreme that they name: `key_cache`: keys of order one; a sequence's first block may hold much larger ones. `key_blocks`: for query block b of sequence s, entries 0 to 2 name key blocks 16 - 4 + b - 2, 12 + b - 1 and 12 + b; entries 3 and 4 name blocks 0 and 1; the last 3 entries are random blocks. Counting the random entries of a sequence over its query blocks in order as t = 0, 1, ..., the t-th lies in blocks k * 2 to (k+1) * 2 - 1 with k = 1 + t mod (6); entries may repeat.
All inputs are finite; a program needn't handle non-finite values.
Results may differ from a plain program's by a relative error of at most 0.018.
Values may be sent and summed in bfloat16 or wider, within the bound.
No kernel may reach another device: no remote copies, remote signals or barrier semaphores. Data moves between devices by JAX's collectives and lax.ppermute only.
A program may use at most 128 MiB of HBM per device.

v0:
```python
import jax
import jax.numpy as jnp
from jax import lax
from jax.sharding import PartitionSpec as P

HEAD = 128
BLOCK = 128
rope_base = 1000000.0


def rotate(vectors, positions):
    half_width = vectors.shape[-1] // 2
    frequency = rope_base ** (
        -(jnp.arange(half_width, dtype=jnp.float32) * 2.0) / vectors.shape[-1]
    )
    angles = positions.astype(jnp.float32)[:, None] * frequency[None, :]
    cosine_table = jnp.cos(angles)[:, None, :]
    sine_table = jnp.sin(angles)[:, None, :]
    front_half = vectors[..., :half_width]
    back_half = vectors[..., half_width:]
    return jnp.concatenate(
        [
            front_half * cosine_table - back_half * sine_table,
            back_half * cosine_table + front_half * sine_table,
        ],
        axis=-1,
    )


def body(tokens, wq, wo, key_cache, value_cache, key_blocks):
    ctx_count = lax.axis_size("ctx")
    row_count = tokens.shape[0]
    query_cols = wq.shape[1]
    projected = jnp.dot(
        tokens, lax.all_gather(wq, "fsdp", axis=0, tiled=True), preferred_element_type=jnp.float32
    )
    cache_count = key_cache.shape[0]
    key_total = cache_count * ctx_count
    positions = key_total - row_count + jnp.arange(row_count, dtype=jnp.int32)
    query = (
        rotate(projected.reshape(row_count, query_cols // HEAD, HEAD), positions) * HEAD ** (-0.5)
    ).astype(jnp.bfloat16)
    kv_cols = key_cache.shape[1] // ctx_count
    keys_whole, values_whole = (
        lax.all_gather(key_cache, "ctx", axis=0, tiled=True),
        lax.all_gather(value_cache, "ctx", axis=0, tiled=True),
    )
    first_col = lax.axis_index("ctx") * kv_cols
    keys_all = lax.dynamic_slice_in_dim(keys_whole, first_col, kv_cols, 1)
    values_all = lax.dynamic_slice_in_dim(values_whole, first_col, kv_cols, 1)
    kv_local = kv_cols // HEAD
    group_size = query_cols // kv_cols
    block_count = key_total // BLOCK
    query_blocks = row_count // BLOCK
    lists = key_blocks[0]
    picked_keys = jnp.take(keys_all.reshape(block_count, BLOCK, kv_local, HEAD), lists, axis=0)
    picked_values = jnp.take(values_all.reshape(block_count, BLOCK, kv_local, HEAD), lists, axis=0)
    shaped = query.reshape(query_blocks, BLOCK, kv_local, group_size, HEAD)
    scores = jnp.einsum(
        "bqkgd,bnskd->bkgqns", shaped, picked_keys, preferred_element_type=jnp.float32
    )
    own_block = block_count - query_blocks + jnp.arange(query_blocks, dtype=jnp.int32)
    own = lists == own_block[:, None]
    causal = jnp.arange(BLOCK)[None, :] <= jnp.arange(BLOCK)[:, None]
    allowed = jnp.logical_or(
        jnp.logical_not(own)[:, None, None, None, :, None], causal[None, None, None, :, None, :]
    )
    scores = jnp.where(allowed, scores, -jnp.inf)
    top_score = jnp.max(scores, axis=(4, 5), keepdims=True)
    raised = jnp.exp(scores - top_score)
    weights = (raised / jnp.sum(raised, axis=(4, 5), keepdims=True)).astype(jnp.bfloat16)
    context = jnp.einsum(
        "bkgqns,bnskd->bqkgd", weights, picked_values, preferred_element_type=jnp.float32
    )
    context = context.astype(jnp.bfloat16).reshape(row_count, query_cols)
    share_terms = jnp.dot(
        context, lax.all_gather(wo, "fsdp", axis=1, tiled=True), preferred_element_type=jnp.float32
    )
    return lax.psum_scatter(
        share_terms.astype(jnp.bfloat16), "ctx", scatter_dimension=1, tiled=True
    )


def solution(mesh):
    in_specs = (
        P("fsdp", None),
        P("fsdp", "ctx"),
        P("ctx", "fsdp"),
        P(("fsdp", "ctx"), None),
        P(("fsdp", "ctx"), None),
        P("fsdp", None, None),
    )
    out_specs = P("fsdp", "ctx")
    return jax.shard_map(body, mesh=mesh, in_specs=in_specs, out_specs=out_specs, check_vma=False)
```

profile of v0, /device:TPU:1, one launch (start us, length us, event | category | flops | bytes accessed | tf_op | source)
XLA Modules:
  0.0 360.2 jit_solution(5195303256417563035)
XLA Ops:
  6.5 0.7 all-gather.5.cloned.1.call-update
  7.3 0.0 all-gather.7.cloned.1.call-start
  7.3 0.7 all-gather.7.cloned.1.call-update
  8.1 0.7 all-gather.9.cloned.1.call-update
  8.7 0.0 all-gather.11.cloned.1.call-start
  8.8 0.5 all-gather.11.cloned.1.call-update
  9.3 0.0 reduce-scatter.2.cloned.1.call-start
  9.4 0.7 compare_select_fusion
  10.1 0.1 reshape.192
  10.2 0.8 fusion.28
  11.0 0.5 multiply_cosine_fusion
  11.5 0.3 broadcast_or_fusion
  11.8 56.0 %all-gather.5.cloned.1.call-done = bf16[2048,1024]{1,0:T(8,128)(2,1)} async-done(((bf16[256,1024]{1,0:T(8,128)(2,1)}), bf16[2048,1024]{1,0:T(8,128)(2,1)}) %all-gather.5.cloned.1.call-update) | async-done | bytes 4194320 | tf_op jit(solution)/shard_map/all_gather | solution.py:46
  67.8 55.2 %all-gather.7.cloned.1.call-done = bf16[2048,1024]{1,0:T(8,128)(2,1)} async-done(((bf16[256,1024]{1,0:T(8,128)(2,1)}), bf16[2048,1024]{1,0:T(8,128)(2,1)}) %all-gather.7.cloned.1.call-update) | async-done | bytes 4194320 | tf_op jit(solution)/shard_map/all_gather | solution.py:45
  123.0 1.3 constant_dynamic-slice_fusion
  124.3 0.7 gather_fusion.1
  125.1 0.7 gather_fusion
  125.8 1.3 copy.8
  127.2 55.4 %all-gather.9.cloned.1.call-done = bf16[8192,512]{1,0:T(8,128)(2,1)} async-done(((bf16[256,512]{1,0:T(8,128)(2,1)}), bf16[8192,512]{1,0:T(8,128)(2,1)}) %all-gather.9.cloned.1.call-update) | async-done | bytes 8388624 | tf_op jit(solution)/shard_map/all_gather | solution.py:35
  182.6 9.4 %fusion.34 = f32[512,512]{0,1:T(8,128)S(1)} fusion(bf16[512,8192]{1,0:T(8,128)(2,1)} %param.8, bf16[8192,512]{1,0:T(8,128)(2,1)} %all-gather.9.cloned.1.call-done), kind=kOutput, calls=%fused_computation.49 | convolution fusion | flops 4294967296 | bytes 17825792 | tf_op jit(solution)/shard_map/dot_general | solution.py:34
  192.0 1.0 multiply_subtract_fusion
  193.0 0.2 concatenate.10
  193.2 0.3 copy.10
  193.5 1.2 concatenate.9
  194.7 1.3 copy.9
  196.0 2.7 fusion
  198.7 1.7 fusion.1
  200.5 2.2 fusion.10
  202.7 0.3 copy.12
  203.0 46.1 %all-gather.11.cloned.1.call-done = bf16[512,8192]{1,0:T(8,128)(2,1)} async-done(((bf16[512,256]{1,0:T(8,128)(2,1)}), bf16[512,8192]{1,0:T(8,128)(2,1)}) %all-gather.11.cloned.1.call-update) | async-done | bytes 8388624 | tf_op jit(solution)/shard_map/all_gather | solution.py:77
  249.1 10.0 %convolution_convert_fusion = bf16[512,8192]{1,0:T(8,128)(2,1)} fusion(bf16[512,8192]{1,0:T(8,128)(2,1)} %all-gather.11.cloned.1.call-done, bf16[64,8,4,128]{3,2,1,0:T(4,128)(2,1)S(1)} %bitcast.100), kind=kOutput, calls=%fused_computation.2 | convolution fusion | flops 4299161600 | bytes 17301504 | tf_op jit(solution)/shard_map/dot_general | solution.py:76
  259.2 94.5 %reduce-scatter.2.cloned.1.call-done = bf16[512,1024]{1,0:T(8,128)(2,1)} async-done(((bf16[512,8192]{1,0:T(8,128)(2,1)}), bf16[512,1024]{1,0:T(8,128)(2,1)}) %reduce-scatter.2.cloned.1.call-update) | async-done | bytes 1048592 | tf_op jit(solution)/shard_map/reduce_scatter | solution.py:79
  (10 shorter events, 0.1 us)
Async XLA Ops:
  6.5 61.3 %all-gather.5.cloned.1.call-start = ((), (), s32[]{:S(2)}) async-start(), calls=%async_computation.1 | async-start | bytes 4718592 | tf_op jit(solution)/shard_map/all_gather | solution.py:46
  7.3 115.8 %all-gather.7.cloned.1.call-start = ((), (), s32[]{:S(2)}) async-start(), calls=%async_computation.2 | async-start | bytes 4718592 | tf_op jit(solution)/shard_map/all_gather | solution.py:45
  8.0 174.6 %all-gather.9.cloned.1.call-start = ((), (), s32[]{:S(2)}) async-start(), calls=%async_computation.3 | async-start | bytes 8650752 | tf_op jit(solution)/shard_map/all_gather | solution.py:35
  8.7 240.4 %all-gather.11.cloned.1.call-start = ((), (), s32[]{:S(2)}) async-start(), calls=%async_computation.4 | async-start | bytes 8650752 | tf_op jit(solution)/shard_map/all_gather | solution.py:77
  9.3 344.3 %reduce-scatter.2.cloned.1.call-start = ((), (), s32[]{:S(2)}) async-start(), calls=%async_computation.5 | async-start | bytes 9437184 | tf_op jit(solution)/shard_map/reduce_scatter | solution.py:79
  198.7 1.8 copy-start
Sparse Core Ops, SparseCore 0:
  9.1 58.6 all-gather.4
  69.6 53.4 all-gather.6
  125.6 56.9 all-gather.8
  184.9 64.1 all-gather.10
  259.3 94.2 reduce-scatter.1
where the time goes:
time: 360 us
  waiting for transfers between devices  310 us (86%)
  matrix products  24.3 us (7%)
  between operations  13.3 us (4%)
  local copies, waits for them, and re-layouts  7.56 us (2%)
  other arithmetic  5.01 us (1%)
    reduce_scatter x1, waiting for transfers between devices, body(): lax.psum_scatter(share_terms.astype(jnp.bfloat16), 'ctx', scatter_dimensi...  94.5 us
    all_gather x1, waiting for transfers between devices, body(): lax.all_gather(value_cache, 'ctx', axis=0, tiled=True)  56 us
    all_gather x1, waiting for transfers between devices, body(): lax.all_gather(wq, 'fsdp', axis=0, tiled=True)  55.4 us
    all_gather x1, waiting for transfers between devices, body(): lax.all_gather(key_cache, 'ctx', axis=0, tiled=True)  55.2 us
    all_gather x1, waiting for transfers between devices, body(): lax.all_gather(wo, 'fsdp', axis=1, tiled=True)  46.1 us
    dot_general x1, matrix products, body(): jnp.dot(context, lax.all_gather(wo, 'fsdp', axis=1, tiled=True), preferre...  10 us
    dot_general x1, matrix products, body(): jnp.dot(tokens, lax.all_gather(wq, 'fsdp', axis=0, tiled=True), preferred...  9.44 us
  transfers between devices with their start and end apart: 5, of which 5 were waited for; matrix products, arithmetic and copies ran while one was open for 7% of the time, Pallas kernels for 0%

commit v1 on v0

--- a/solution.py
+++ b/solution.py
@@ -42,7 +42,9 @@
     ).astype(jnp.bfloat16)
     kv_cols = key_cache.shape[1] // ctx_count
     keys_whole, values_whole = (
-        lax.all_gather(key_cache, "ctx", axis=0, tiled=True),
+        jnp.concatenate(
+            lax.all_to_all(jnp.stack([key_cache] * lax.axis_size("ctx")), "ctx", 0, 0), axis=0
+        ),
         lax.all_gather(value_cache, "ctx", axis=0, tiled=True),
     )
     first_col = lax.axis_index("ctx") * kv_cols

time: 360 us -> 393 us (1.092)
  waiting for transfers between devices: 310 us -> 331 us
  starting transfers between devices: 0.15 us -> 9.13 us
    all_to_all x0 -> x1, waiting for transfers between devices: none -> 135 us  [body(): lax.all_to_all(jnp.stack([key_cache] * lax.axis_size('ctx')), 'ctx', 0, 0)]
    all_gather x1, waiting for transfers between devices: 56 us -> 0.01 us  [body(): lax.all_gather(value_cache, 'ctx', axis=0, tiled=True)]
    all_gather x1 -> x0, waiting for transfers between devices: 55.2 us -> none  [body(): lax.all_gather(key_cache, 'ctx', axis=0, tiled=True)]
    all_to_all x0 -> x1, starting transfers between devices: none -> 9.01 us  [body(): lax.all_to_all(jnp.stack([key_cache] * lax.axis_size('ctx')), 'ctx', 0, 0)]
  transfers between devices with their start and end apart: 5 -> 5, of which waited for: 5 -> 4; matrix products, arithmetic and copies ran while one was open for 7% -> 7% of each run, Pallas kernels for 0% -> 0%
where the time goes in v1:
time: 393 us
  waiting for transfers between devices  331 us (84%)
  matrix products  24.3 us (6%)
  between operations  13.3 us (3%)
  local copies, waits for them, and re-layouts  11.1 us (3%)
  starting transfers between devices  9.13 us (2%)
    all_to_all x1, waiting for transfers between devices, body(): lax.all_to_all(jnp.stack([key_cache] * lax.axis_size('ctx')), 'ctx', 0, 0)  135 us
    reduce_scatter x1, waiting for transfers between devices, body(): lax.psum_scatter(share_terms.astype(jnp.bfloat16), 'ctx', scatter_dimensi...  94.5 us
    all_gather x1, waiting for transfers between devices, body(): lax.all_gather(wq, 'fsdp', axis=0, tiled=True)  53.5 us
    all_gather x1, waiting for transfers between devices, body(): lax.all_gather(wo, 'fsdp', axis=1, tiled=True)  46.3 us
    dot_general x1, matrix products, body(): jnp.dot(context, lax.all_gather(wo, 'fsdp', axis=1, tiled=True), preferre...  10 us
    dot_general x1, matrix products, body(): jnp.dot(tokens, lax.all_gather(wq, 'fsdp', axis=0, tiled=True), preferred...  9.44 us
    all_to_all x1, starting transfers between devices, body(): lax.all_to_all(jnp.stack([key_cache] * lax.axis_size('ctx')), 'ctx', 0, 0)  9.01 us
  transfers between devices with their start and end apart: 5, of which 4 were waited for; matrix products, arithmetic and copies ran while one was open for 7% of the time, Pallas kernels for 0%

profile of v1, /device:TPU:1, one launch (start us, length us, event | category | flops | bytes accessed | tf_op | source)
XLA Modules:
  0.0 392.7 jit_solution(14830312158128635908)
XLA Ops:
  6.5 0.7 all-gather.4.cloned.1.call-update
  7.3 0.0 all-gather.6.cloned.1.call-start
  7.3 0.7 all-gather.6.cloned.1.call-update
  8.0 0.0 all-gather.8.cloned.1.call-start
  8.1 0.7 all-gather.8.cloned.1.call-update
  8.7 3.5 stack.2
  12.3 9.0 %all-to-all-start = ((bf16[8,256,1024]{2,1,0:T(8,128)(2,1)}), bf16[8,256,1024]{2,1,0:T(8,128)(2,1)}, u32[]{:S(2)}, u32[]{:S(2)}) async-start(bf16[8,256,1024]{2,1,0:T(8,128)(2,1)} %stack.2), calls=%async_computation | async-start | bytes 8388608 | tf_op jit(solution)/shard_map/all_to_all | solution.py:46
  21.3 0.0 reduce-scatter.2.cloned.1.call-start
  21.4 0.1 reshape.198
  21.5 0.1 fusion.28
  21.6 0.5 multiply_cosine_fusion
  22.1 0.3 broadcast_or_fusion
  22.4 134.9 %all-to-all-done = bf16[8,256,1024]{2,1,0:T(8,128)(2,1)} async-done(((bf16[8,256,1024]{2,1,0:T(8,128)(2,1)}), bf16[8,256,1024]{2,1,0:T(8,128)(2,1)}, u32[]{:S(2)}, u32[]{:S(2)}) %all-to-all-start) | async-done | bytes 4194336 | tf_op jit(solution)/shard_map/all_to_all | solution.py:46
  157.3 1.3 constant_dynamic-slice_fusion
  158.6 0.7 gather_fusion.1
  159.4 0.7 gather_fusion
  160.1 1.3 copy.8
  161.5 53.5 %all-gather.6.cloned.1.call-done = bf16[8192,512]{1,0:T(8,128)(2,1)} async-done(((bf16[256,512]{1,0:T(8,128)(2,1)}), bf16[8192,512]{1,0:T(8,128)(2,1)}) %all-gather.6.cloned.1.call-update) | async-done | bytes 8388624 | tf_op jit(solution)/shard_map/all_gather | solution.py:35
  214.9 9.4 %fusion.34 = f32[512,512]{0,1:T(8,128)S(1)} fusion(bf16[512,8192]{1,0:T(8,128)(2,1)} %param.8, bf16[8192,512]{1,0:T(8,128)(2,1)} %all-gather.6.cloned.1.call-done), kind=kOutput, calls=%fused_computation.49 | convolution fusion | flops 4294967296 | bytes 17825792 | tf_op jit(solution)/shard_map/dot_general | solution.py:34
  224.4 1.0 multiply_subtract_fusion
  225.3 0.2 concatenate.10
  225.5 0.3 copy.10
  225.9 1.2 concatenate.9
  227.1 1.3 copy.9
  228.4 2.7 fusion
  231.1 1.7 fusion.1
  232.8 2.2 fusion.10
  235.1 0.3 copy.12
  235.4 46.3 %all-gather.8.cloned.1.call-done = bf16[512,8192]{1,0:T(8,128)(2,1)} async-done(((bf16[512,256]{1,0:T(8,128)(2,1)}), bf16[512,8192]{1,0:T(8,128)(2,1)}) %all-gather.8.cloned.1.call-update) | async-done | bytes 8388624 | tf_op jit(solution)/shard_map/all_gather | solution.py:79
  281.6 10.0 %convolution_convert_fusion = bf16[512,8192]{1,0:T(8,128)(2,1)} fusion(bf16[512,8192]{1,0:T(8,128)(2,1)} %all-gather.8.cloned.1.call-done, bf16[64,8,4,128]{3,2,1,0:T(4,128)(2,1)S(1)} %bitcast.101), kind=kOutput, calls=%fused_computation.2 | convolution fusion | flops 4299161600 | bytes 17301504 | tf_op jit(solution)/shard_map/dot_general | solution.py:78
  291.7 0.0 reduce-scatter.2.cloned.1.call-update
  291.7 94.5 %reduce-scatter.2.cloned.1.call-done = bf16[512,1024]{1,0:T(8,128)(2,1)} async-done(((bf16[512,8192]{1,0:T(8,128)(2,1)}), bf16[512,1024]{1,0:T(8,128)(2,1)}) %reduce-scatter.2.cloned.1.call-update) | async-done | bytes 1048592 | tf_op jit(solution)/shard_map/reduce_scatter | solution.py:81
  (12 shorter events, 0.1 us)
Async XLA Ops:
  6.5 14.8 %copy-start.1 = (s32[1,4,8]{2,1,0:T(4,128)S(1)}, s32[1,4,8]{2,1,0:T(4,128)}, u32[]{:S(2)}) copy-start(s32[1,4,8]{2,1,0:T(4,128)} %param.13) | copy-start | bytes 388
  6.5 150.8 %all-gather.4.cloned.1.call-start = ((), (), s32[]{:S(2)}) async-start(), calls=%async_computation.2 | async-start | bytes 4718592 | tf_op jit(solution)/shard_map/all_gather | solution.py:48
  7.3 207.7 %all-gather.6.cloned.1.call-start = ((), (), s32[]{:S(2)}) async-start(), calls=%async_computation.3 | async-start | bytes 8650752 | tf_op jit(solution)/shard_map/all_gather | solution.py:35
  8.0 273.6 %all-gather.8.cloned.1.call-start = ((), (), s32[]{:S(2)}) async-start(), calls=%async_computation.4 | async-start | bytes 8650752 | tf_op jit(solution)/shard_map/all_gather | solution.py:79
  12.3 145.0 %all-to-all-start = ((bf16[8,256,1024]{2,1,0:T(8,128)(2,1)}), bf16[8,256,1024]{2,1,0:T(8,128)(2,1)}, u32[]{:S(2)}, u32[]{:S(2)}) async-start(bf16[8,256,1024]{2,1,0:T(8,128)(2,1)} %stack.2), calls=%async_computation | async-start | bytes 8388608 | tf_op jit(solution)/shard_map/all_to_all | solution.py:46
  21.3 364.9 %reduce-scatter.2.cloned.1.call-start = ((), (), s32[]{:S(2)}) async-start(), calls=%async_computation.5 | async-start | bytes 9437184 | tf_op jit(solution)/shard_map/reduce_scatter | solution.py:81
  231.1 1.8 copy-start
Sparse Core Ops, SparseCore 0:
  9.1 143.2 all-gather.3
  155.0 59.8 all-gather.5
  217.4 64.1 all-gather.7
  291.8 94.2 reduce-scatter.1
